TPU v7x, 512 devices: a whole 4x4x16 slice. The times are simulated.
512 devices in a mesh: row: 32 (over z, core), col: 16 (over y, x).
Axes of the slice: x: 4, y: 4, z: 16, core: 2. Of those that a mesh axis runs over, the one named last changes fastest.
Arguments:
- example_sketch: float32 [512, 32768], P('col', 'row'), may hold values from -6 to 6
- candidate_sketch: float32 [512, 32768], P('row', 'col'), may hold values from -6 to 6
- best_start: float32 [32768], P('row'), may hold values from -1 to 1.5
- chosen: int32 [2], replicated, may hold values from 0 to 32767
Outputs:
- best: float32 [32768], P('row')
- gains: float32 [2, 32768], P(None, 'col')
All inputs are finite; a program needn't handle non-finite values.
Results may differ from a plain program's by a relative error of at most 0.000075.
Values sent between devices are 32-bit elements; how exact they have to be, the bound alone decides.
A program may use at most 64 MiB of HBM per device.

v0:
```python
import jax
import jax.numpy as jnp
from jax import lax
from jax.sharding import Mesh
from jax.sharding import PartitionSpec as P

COL = ("col_0", "col_1")


EPS = 1e-06


def from_everyone(array, axis):
    copies = jnp.broadcast_to(array, (lax.axis_size(axis), *array.shape))
    return lax.all_to_all(copies, axis, split_axis=0, concat_axis=0, tiled=True)


def joined_along(blocks, dim):
    blocks = jnp.moveaxis(blocks, 0, dim)
    dims = blocks.shape
    return blocks.reshape(*dims[:dim], dims[dim] * dims[dim + 1], *dims[dim + 2 :])


def gather_directly(array, axis, dim):
    blocks = from_everyone(array, axis)
    return joined_along(blocks, dim)


def broadcast_by_axis(array, axes, root):
    array = jnp.where(lax.axis_index(axes) == root, array, jnp.zeros_like(array))
    for axis in axes:
        array = lax.psum(array, axis)
    return array


def taken_together(array, axis):
    everything = from_everyone(array, axis)
    return jnp.sum(everything, axis=0)


def on_device(example_sketch, candidate_sketch, best_start, chosen):
    examples_full = gather_directly(example_sketch, COL, 0)
    cand_full = lax.all_gather(candidate_sketch, "row", axis=0, tiled=True)
    width = examples_full.shape[0]
    scale = jnp.sqrt(jnp.float32(width))
    ex_sq = jnp.sum(examples_full * examples_full, axis=0)
    cand_sq = jnp.sum(cand_full * cand_full, axis=0)
    ex_norm = jnp.sqrt(ex_sq + EPS)
    cand_norm = jnp.sqrt(cand_sq + EPS)
    factor = scale / ex_norm
    dots = lax.dot_general(
        examples_full,
        cand_full,
        (((0,), (0,)), ((), ())),
        precision=lax.Precision.HIGHEST,
        preferred_element_type=jnp.float32,
    )
    similar = dots * factor[:, None] / cand_norm[None, :]
    c_local = similar.shape[1]
    total_examples = similar.shape[0] * lax.axis_size("row")
    best = best_start
    partials = []
    for step in range(chosen.shape[0]):
        pick = chosen[step]
        owner = pick // c_local
        offset = pick % c_local
        column = lax.dynamic_slice_in_dim(similar, offset, 1, 1)[:, 0]
        column = broadcast_by_axis(column, COL, owner)
        best = jnp.maximum(best, column)
        local_gain = jnp.sum(jnp.maximum(similar - best[:, None], 0.0), axis=0)
        partials.append(local_gain)
    gains = taken_together(jnp.stack(partials), "row") / total_examples
    return (best, gains)


def solution(mesh):
    split = Mesh(mesh.devices.reshape(mesh.shape["row"], 4, 4), ("row", "col_0", "col_1"))
    return jax.shard_map(
        on_device,
        mesh=split,
        in_specs=(P(COL, "row"), P("row", COL), P("row"), P()),
        out_specs=(P("row"), P(None, COL)),
        check_vma=False,
    )
```

profile of v0, /device:TPU:1, one launch (start us, length us, event | category | flops | bytes accessed | tf_op | source)
XLA Modules:
  0.0 187.4 jit_solution(15693712530953939537)
XLA Ops:
  7.2 0.0 all-gather.2.cloned.1.call-start
  7.2 0.7 all-gather.2.cloned.1.call-update
  7.9 2.5 %broadcast_in_dim.4 = f32[16,32,1024]{2,1,0:T(8,128)} broadcast(f32[32,1024]{1,0:T(8,128)} %param.4), dimensions={1,2} | broadcast | bytes 2228224 | tf_op jit(solution)/shard_map/broadcast_in_dim | solution.py:14
  10.4 7.6 %all-to-all-start = ((f32[16,32,1024]{2,1,0:T(8,128)}), f32[16,32,1024]{2,1,0:T(8,128)S(1)}, u32[]{:S(2)}, u32[]{:S(2)}) async-start(f32[16,32,1024]{2,1,0:T(8,128)} %broadcast_in_dim.4), calls=%async_computation | async-start | bytes 4194304 | tf_op jit(solution)/shard_map/all_to_all | solution.py:15
  18.0 1.3 fusion.1
  24.5 18.6 %all-to-all-done = f32[16,32,1024]{2,1,0:T(8,128)S(1)} async-done(((f32[16,32,1024]{2,1,0:T(8,128)}), f32[16,32,1024]{2,1,0:T(8,128)S(1)}, u32[]{:S(2)}, u32[]{:S(2)}) %all-to-all-start) | async-done | bytes 2097184 | tf_op jit(solution)/shard_map/all_to_all | solution.py:15
  43.2 0.2 multiply_reduce_fusion.1
  43.4 46.6 %all-gather.2.cloned.1.call-done = f32[512,2048]{1,0:T(8,128)} async-done(((f32[16,2048]{1,0:T(8,128)}), f32[512,2048]{1,0:T(8,128)}) %all-gather.2.cloned.1.call-update) | async-done | bytes 4194320 | tf_op jit(solution)/shard_map/all_gather | solution.py:43
  90.0 2.6 %multiply_reduce_fusion = f32[2048]{0:T(1024)S(1)} fusion(f32[512,2048]{1,0:T(8,128)} %all-gather.2.cloned.1.call-done), kind=kLoop, calls=%fused_computation.3 | loop fusion | flops 2095104 | bytes 4202496 | tf_op jit(solution)/shard_map/reduce_sum | solution.py:47
  92.5 0.0 copy-start.2
  92.5 16.3 %multiply_divide_fusion = f32[1024,2048]{1,0:T(8,128)S(1)} fusion(f32[512,1024]{1,0:T(8,128)S(1)} %bitcast.7, f32[512,2048]{1,0:T(8,128)} %all-gather.2.cloned.1.call-done, f32[2048]{0:T(1024)S(1)} %add_sqrt_fusion, f32[1024]{0:T(1024)S(1)} %rsqrt_multiply_fusion), kind=kOutput, calls=%fused_computation.2 | convolution fusion | flops 12889096192 | bytes 14692352 | tf_op jit(solution)/shard_map/dot_general | solution.py:51
  108.9 0.0 copy-start
  108.9 3.2 %copy-done = f32[1024,2048]{1,0:T(8,128)} copy-done((f32[1024,2048]{1,0:T(8,128)}, f32[1024,2048]{1,0:T(8,128)S(1)}, u32[]{:S(2)}) %copy-start) | copy-done | bytes 8388632
  112.1 0.6 select_reduce_fusion
  112.7 8.7 %all-reduce.1 = (f32[1024]{0:T(1024)S(1)}, f32[1024]{0:T(1024)S(1)}) all-reduce(f32[1024]{0:T(1024)S(1)} %get-tuple-element.5, f32[1024]{0:T(1024)S(1)} %get-tuple-element.4), channel_id=1, replica_groups=mesh['row'=32,'col_0'=4,'col_1'=4] {'col_0'}, use_global_device_ids=true, to_apply=%region_2.3 | all-reduce | flops 2048 | bytes 16384 | tf_op jit(solution)/shard_map/psum | solution.py:32
  121.4 8.3 %all-reduce = (f32[1024]{0:T(1024)S(1)}, f32[1024]{0:T(1024)S(1)}) all-reduce(f32[1024]{0:T(1024)S(1)} %get-tuple-element.8, f32[1024]{0:T(1024)S(1)} %get-tuple-element.9), channel_id=1, replica_groups=mesh['row'=32,'col_0'=4,'col_1'=4] {'col_1'}, use_global_device_ids=true, to_apply=%region_3.4 | all-reduce | flops 2048 | bytes 16384 | tf_op jit(solution)/shard_map/psum | solution.py:32
  129.7 0.0 copy-done.2
  129.8 0.0 copy-start.1
  129.8 4.4 %maximum_reduce_fusion.1 = (f32[2048]{0:T(1024)S(1)}, f32[2048]{0:T(1024)S(1)}) fusion(f32[1024,2048]{1,0:T(8,128)} %copy-done, f32[1024]{0:T(1024)S(1)} %get-tuple-element.11, f32[1024]{0:T(1024)S(1)} %get-tuple-element.10), kind=kLoop, calls=%fused_computation.1 | loop fusion | flops 12578816 | bytes 8413184 | tf_op jit(solution)/shard_map/reduce_sum | solution.py:70
  134.2 0.2 broadcast_in_dim.5
  134.4 45.3 %all_to_all.10 = f32[32,2,2048]{2,1,0:T(2,128)S(1)} all-to-all(f32[32,2,2048]{2,1,0:T(2,128)S(1)} %broadcast_in_dim.5), channel_id=1, replica_groups=mesh['row'=32,'col_0'=4,'col_1'=4] {'row'}, dimensions={0} | all-to-all | bytes 1048576 | tf_op jit(solution)/shard_map/all_to_all | solution.py:15
  179.8 0.2 reduce_sum.49
  179.9 0.6 broadcast_multiply_fusion
  180.5 0.0 copy-done.1
  (4 shorter events, 0.0 us)
Async XLA Ops:
  7.2 82.8 %all-gather.2.cloned.1.call-start = ((), (), s32[]{:S(2)}) async-start(), calls=%async_computation.2 | async-start | bytes 4325376 | tf_op jit(solution)/shard_map/all_gather | solution.py:43
  10.4 32.8 %all-to-all-start = ((f32[16,32,1024]{2,1,0:T(8,128)}), f32[16,32,1024]{2,1,0:T(8,128)S(1)}, u32[]{:S(2)}, u32[]{:S(2)}) async-start(f32[16,32,1024]{2,1,0:T(8,128)} %broadcast_in_dim.4), calls=%async_computation | async-start | bytes 4194304 | tf_op jit(solution)/shard_map/all_to_all | solution.py:15
  92.5 37.2 %copy-start.2 = (f32[1024]{0:T(1024)S(1)}, f32[1024]{0:T(1024)}, u32[]{:S(2)}) copy-start(f32[1024]{0:T(1024)} %param.6) | copy-start | bytes 12292
  108.9 3.2 %copy-start = (f32[1024,2048]{1,0:T(8,128)}, f32[1024,2048]{1,0:T(8,128)S(1)}, u32[]{:S(2)}) copy-start(f32[1024,2048]{1,0:T(8,128)S(1)} %multiply_divide_fusion) | copy-start | bytes 25165828
  129.8 50.8 %copy-start.1 = (f32[1024]{0:T(1024)}, f32[1024]{0:T(1024)S(1)}, u32[]{:S(2)}) copy-start(f32[1024]{0:T(1024)S(1)} %get-tuple-element.10) | copy-start | bytes 12292
Sparse Core Ops, SparseCore 0:
  10.1 79.7 all-gather.1
where the time goes:
time: 188 us; the launch traced here: 187 us
  waiting for transfers between devices  65.9 us (35%)
  blocking collectives  62.3 us (33%)
  between operations  19.4 us (10%)
  matrix products  16.3 us (9%)
  other arithmetic  8.58 us (5%)
  starting transfers between devices  7.62 us (4%)
  local copies, waits for them, and re-layouts  7.25 us (4%)
    all_gather x1, waiting for transfers between devices, on_device(): cand_full = lax.all_gather(candidate_sketch, 'row', axis=0, tiled=True)  46.6 us
    all_to_all x1, blocking collectives, from_everyone(): return lax.all_to_all(copies, axis, split_axis=0, concat_axis=0, tiled=True)  45.3 us
    all_to_all x1, waiting for transfers between devices, from_everyone(): return lax.all_to_all(copies, axis, split_axis=0, concat_axis=0, tiled=True)  18.6 us
    psum x2, blocking collectives, broadcast_by_axis(): array = lax.psum(array, axis)  17 us
    dot_general x1, matrix products, on_device(): lax.dot_general(examples_full, cand_full, (((0,), (0,)), ((), ())), preci...  16.3 us
    all_to_all x1, starting transfers between devices, from_everyone(): return lax.all_to_all(copies, axis, split_axis=0, concat_axis=0, tiled=True)  7.58 us
    reduce_sum x1, other arithmetic, on_device(): local_gain = jnp.sum(jnp.maximum(similar - best[:, None], 0.0), axis=0)  4.39 us
  transfers between devices with their start and end apart: 2, of which 2 were waited for; matrix products, arithmetic and copies ran while one was open for 2% of the time, Pallas kernels for 0%

commit v1 on v0

v1 whole, which is shorter than its diff:
```python
import functools

import jax
import jax.numpy as jnp
from jax import lax
from jax.experimental import pallas as pl
from jax.experimental.pallas import tpu as pltpu
from jax.sharding import PartitionSpec as P

EPS = 1e-06
LEVELS = 16
GROUP = 32
PIECES = 4
TILE = 256
F32, BF16 = jnp.float32, jnp.bfloat16


def remote(src, dst, send, recv, row, col):
    return pltpu.make_async_remote_copy(
        src_ref=src,
        dst_ref=dst,
        send_sem=send,
        recv_sem=recv,
        device_id={"row": row, "col": col},
        device_id_type=pl.DeviceIdType.MESH,
    )


def slot_rows(slot):
    return pl.ds((slot % LEVELS) * GROUP, GROUP)


def kernel(
    ex_hbm, cand_hbm, best_ref, chosen_ref, best_out, gains_out,
    cand, c_hi, c_lo, c_sq, ex, e_hi, e_lo, acc, best_rep, ch_part, ch, ch_hi, ch_lo,
    g_own, g_sib, g_all, g_sum,
    loc_sem, ring_s, ring_r, sib_s, sib_r, p1_s, p1_r, p2_s, p2_r,
    cx_s, cx_r, z1_s, z1_r, z2_s, z2_r, gs_s, gs_r, gz_s, gz_r, gf_s, gf_r,
):
    row, col = lax.axis_index("row"), lax.axis_index("col")
    z, c, y, x = row // 2, row % 2, col // 4, col % 4
    xs = [y * 4 + (x + j) % 4 for j in range(1, 4)]
    ys = [((y + j) % 4) * 4 + x for j in range(1, 4)]
    above, below = ((z + 1) % LEVELS) * 2, ((z + LEVELS - 1) % LEVELS) * 2
    sib = z * 2 + 1 - c
    onward = jnp.where(c == 0, above, below + 1)
    pending = []

    def go(*args):
        copy = remote(*args)
        copy.start()
        pending.append(copy)

    def arrived(view, sem):
        remote(view, view, loc_sem.at[0], sem, sib, col).wait_recv()

    mine = pl.ds(pl.multiple_of(4 * GROUP + c * 16, 16), 16)
    ex_slot = (col - z + 4 + LEVELS) % LEVELS
    copy_c = pltpu.make_async_copy(cand_hbm, cand.at[mine], loc_sem.at[0])
    copy_e = pltpu.make_async_copy(
        ex_hbm, ex.at[pl.ds(pl.multiple_of(ex_slot * GROUP, GROUP), GROUP)], loc_sem.at[1]
    )
    copy_c.start()
    copy_e.start()

    barrier = pltpu.get_barrier_semaphore()
    near = [(r, col) for r in (above, above + 1, below, below + 1, sib)]
    near += [(row, t) for t in xs + ys]
    for r, t in near:
        pl.semaphore_signal(
            barrier, inc=1, device_id={"row": r, "col": t}, device_id_type=pl.DeviceIdType.MESH
        )
    pl.semaphore_wait(barrier, len(near))
    copy_c.wait()

    width = cand.shape[1] * 2 // PIECES

    def piece(first_row, half, k):
        start = pl.multiple_of(first_row + 8 * half, 8)
        return cand.at[pl.ds(start, 8), pl.ds((k // 2) * width, width)]

    for k in range(PIECES):
        src = piece(4 * GROUP + c * 16, k % 2, k)
        go(src, piece(3 * GROUP + c * 16, k % 2, k), ring_s.at[0, 0, k], ring_r.at[0, c, k], above, col)
        go(src, piece(5 * GROUP + c * 16, k % 2, k), ring_s.at[0, 1, k], ring_r.at[0, c, k], below + 1, col)
    go(cand.at[mine], cand.at[mine], sib_s.at[0], sib_r.at[0], sib, col)

    copy_e.wait()

    def ex_view(t, half):
        slot = (t - z + 4 + LEVELS) % LEVELS
        return ex.at[pl.ds(pl.multiple_of(slot * GROUP + 16 * half, 16), 16)]

    for j in range(3):
        go(ex_view(col, 0), ex_view(col, 0), p1_s.at[0, j], p1_r.at[0, j], row, xs[j])
        go(ex_view(col, 1), ex_view(col, 1), p1_s.at[1, j], p1_r.at[1, j], row, ys[j])
    for j in range(3):
        go(ex_view(col, 0), ex_view(col, 0), p2_s.at[0, 3, j], p2_r.at[0, 3, j], row, ys[j])
        go(ex_view(col, 1), ex_view(col, 1), p2_s.at[1, 3, j], p2_r.at[1, 3, j], row, xs[j])

    def hop(h):
        base = jnp.where(c == 0, ((4 - h) % LEVELS) * GROUP, ((4 + h) % LEVELS) * GROUP)
        after = jnp.where(c == 0, ((3 - h) % LEVELS) * GROUP, ((5 + h) % LEVELS) * GROUP)
        for k in range(PIECES):
            for o in range(2):
                far = k % 2 == 0
                if h == 8 and not far:
                    continue
                half = (k % 2 + c) % 2
                view = piece(base + o * 16, half, k)
                kk = (k // 2) * 2 + half if h == 1 else k
                arrived(view, ring_r.at[h - 1, o, kk])
                if h < 7 or (far and h < 8):
                    go(view, piece(after + o * 16, half, k), ring_s.at[h, o, k], ring_r.at[h, o, k], onward, col)
        if h < 8:
            view = cand.at[pl.ds(pl.multiple_of(base, GROUP), GROUP)]
            go(view, view, sib_s.at[h], sib_r.at[h], sib, col)
        else:
            for o in range(2):
                view = cand.at[pl.ds(pl.multiple_of(base + o * 16 + 8 * c, 8), 8)]
                go(view, view, sib_s.at[8 + o], sib_r.at[8 + o], sib, col)

    def from_sib(h):
        if h == 0:
            arrived(cand.at[pl.ds(0, 16)], sib_r.at[0])
        elif h < 8:
            arrived(cand.at[pl.ds(0, GROUP)], sib_r.at[h])
        else:
            for o in range(2):
                arrived(cand.at[pl.ds(0, 8)], sib_r.at[8 + o])

    def prepare(slot):
        v = cand[slot_rows(slot), :]
        hi = v.astype(BF16)
        c_hi[slot_rows(slot), :] = hi
        c_lo[slot_rows(slot), :] = (v - hi.astype(F32)).astype(BF16)
        sq = v * v
        c_sq[...] += sq[0:8] + sq[8:16] + sq[16:24] + sq[24:32]

    lane = lax.broadcasted_iota(jnp.int32, (128, 128), 1)
    sub = lax.broadcasted_iota(jnp.int32, (128, 128), 0)

    c_sq[...] = jnp.zeros_like(c_sq)
    for i in range(8):
        best_rep[0, pl.ds(128 * i, 128), :] = jnp.broadcast_to(best_ref[pl.ds(i, 1), :], (128, 128)).T
    from_sib(0)
    level = cand[slot_rows(4), :]
    wide = lax.broadcasted_iota(jnp.int32, level.shape, 1)
    tile = jnp.zeros((8, 128), F32)
    for r in range(2):
        at = chosen_ref[r] - col * level.shape[1]
        value = jnp.sum(jnp.where(wide == at, level, 0.0), axis=1, keepdims=True)
        line = jnp.sum(
            jnp.where(lane[:GROUP] == sub[:GROUP] + GROUP * (z % 4), value, 0.0), axis=0, keepdims=True
        )
        tile = tile + jnp.where(sub[:8] == r, line, 0.0)
    ch_part[0] = tile
    for j in range(3):
        go(ch_part.at[0], ch_part.at[2 + j], cx_s.at[0, j], cx_r.at[0, j], row, xs[j])
    prepare(4)

    hop(1)
    for i in (0, 2, 1):
        bx, by = y * 4 + (x + 3 - i) % 4, ((y + 3 - i) % 4) * 4 + x
        arrived(ex_view(bx, 0), p1_r.at[0, i])
        for j in range(3):
            go(ex_view(bx, 0), ex_view(bx, 0), p2_s.at[0, i, j], p2_r.at[0, i, j], row, ys[j])
        arrived(ex_view(by, 1), p1_r.at[1, i])
        for j in range(3):
            go(ex_view(by, 1), ex_view(by, 1), p2_s.at[1, i, j], p2_r.at[1, i, j], row, xs[j])
    for j in range(3):
        arrived(ch_part.at[2 + j], cx_r.at[0, j])
    ch_part[1] = ch_part[0] + ch_part[2] + ch_part[3] + ch_part[4]
    for j in range(3):
        go(ch_part.at[1], ch_part.at[5 + j], cx_s.at[1, j], cx_r.at[1, j], row, ys[j])
    from_sib(1)
    prepare(3)
    prepare(5)

    hop(2)
    for j in range(3):
        arrived(ch_part.at[5 + j], cx_r.at[1, j])
    ch[4] = ch_part[1] + ch_part[5] + ch_part[6] + ch_part[7]
    from_sib(2)
    prepare(2)
    prepare(6)

    hop(3)
    from_sib(3)
    prepare(1)
    prepare(7)

    hop(4)
    from_sib(4)
    for d in range(1, 5):
        go(ch.at[4], ch.at[4 - d], z1_s.at[0, d - 1], z1_r.at[0, d - 1], ((z + d) % LEVELS) * 2 + c, col)
        go(ch.at[4], ch.at[4 + d], z1_s.at[1, d - 1], z1_r.at[1, d - 1], ((z + LEVELS - d) % LEVELS) * 2 + c, col)
    prepare(0)
    prepare(8)

    hop(5)
    for half in range(2):
        for i in range(4):
            for j in range(3):
                arrived(ex.at[pl.ds(0, 16)], p2_r.at[half, i, j])
    e_sq = jnp.zeros((8, ex.shape[1]), F32)
    for i in range(64):
        v = ex[pl.ds(8 * i, 8), :]
        e_sq = e_sq + v * v
    factor = jnp.sqrt(jnp.float32(LEVELS * GROUP)) / jnp.sqrt(jnp.sum(e_sq, axis=0, keepdims=True) + EPS)
    from_sib(5)
    for d in range(1, 5):
        arrived(ch.at[0], z1_r.at[0, d - 1])
        arrived(ch.at[0], z1_r.at[1, d - 1])
    go(ch.at[pl.ds(0, 4)], ch.at[pl.ds(12, 4)], z2_s.at[0], z2_r.at[0], ((z + 4) % LEVELS) * 2 + c, col)
    go(ch.at[pl.ds(5, 3)], ch.at[pl.ds(9, 3)], z2_s.at[1], z2_r.at[1], ((z + LEVELS - 4) % LEVELS) * 2 + c, col)
    prepare(15)
    prepare(9)

    hop(6)
    for i in range(8):
        for q in range(4):
            block = ex[pl.ds(128 * q, 128), pl.ds(128 * i, 128)] * factor[:, 128 * i : 128 * (i + 1)]
            block = block.T
            hi = block.astype(BF16)
            e_hi[pl.ds(128 * i, 128), pl.ds(128 * q, 128)] = hi
            e_lo[pl.ds(128 * i, 128), pl.ds(128 * q, 128)] = (block - hi.astype(F32)).astype(BF16)
    from_sib(6)
    prepare(14)
    prepare(10)

    def product(first, hi, lo):
        a_hi, a_lo = e_hi[:, pl.ds(first, 256)], e_lo[:, pl.ds(first, 256)]
        dot = functools.partial(jnp.dot, preferred_element_type=F32)
        return dot(a_hi, hi) + dot(a_lo, hi) + dot(a_hi, lo)

    hop(7)
    arrived(ch.at[pl.ds(0, 4)], z2_r.at[0])
    arrived(ch.at[pl.ds(0, 3)], z2_r.at[1])
    ch_sq = [jnp.zeros((1, 128), F32), jnp.zeros((1, 128), F32)]
    for q in range(4):
        four = ch[4 * q] + ch[4 * q + 1] + ch[4 * q + 2] + ch[4 * q + 3]
        for r in range(2):
            v = jnp.broadcast_to(four[r : r + 1, :], (128, 128)).T
            ch_sq[r] = ch_sq[r] + jnp.sum(v * v, axis=0, keepdims=True)
            hi = v.astype(BF16)
            lo = (v - hi.astype(F32)).astype(BF16)
            for b in range(4):
                to = pl.ds(pl.multiple_of(((b - z + LEVELS) % 4 + 4 * q) * GROUP, GROUP), GROUP)
                ch_hi[to, pl.ds(128 * r, 128)] = hi[32 * b : 32 * b + 32]
                ch_lo[to, pl.ds(128 * r, 128)] = lo[32 * b : 32 * b + 32]

    def pick(i, _):
        rows = pl.ds(pl.multiple_of(i * 128, 128), 128)
        dot = functools.partial(jnp.dot, preferred_element_type=F32)
        hi, lo = e_hi[rows, :], e_lo[rows, :]
        d = dot(hi, ch_hi[...]) + dot(lo, ch_hi[...]) + dot(hi, ch_lo[...])
        b = best_rep[0, rows, :]
        for r in range(2):
            b = jnp.maximum(b, d[:, 128 * r : 128 * r + 128] / jnp.sqrt(ch_sq[r] + EPS))
            best_rep[r, rows, :] = b
        best_out[pl.ds(i, 1), :] = jnp.sum(jnp.where(lane == sub, b, 0.0), axis=0, keepdims=True)
        return 0

    lax.fori_loop(0, 8, pick, 0)

    def first_half(n, _):
        cols = pl.ds(pl.multiple_of(n * TILE, TILE), TILE)
        acc[:, cols] = product(0, c_hi[pl.ds(0, 256), cols], c_lo[pl.ds(0, 256), cols])
        return 0

    lax.fori_loop(0, 8, first_half, 0)
    from_sib(7)
    prepare(13)
    prepare(11)

    hop(8)
    from_sib(8)
    prepare(12)

    def second_half(n, _):
        cols = pl.ds(pl.multiple_of(n * TILE, TILE), TILE)
        d = acc[:, cols] + product(256, c_hi[pl.ds(256, 256), cols], c_lo[pl.ds(256, 256), cols])
        norm = jnp.sqrt(jnp.sum(c_sq[:, cols], axis=0, keepdims=True) + EPS)
        sim = d * (1.0 / norm)
        for r in range(2):
            b = best_rep[r]
            for t in range(2):
                part = jnp.maximum(sim[:, 128 * t : 128 * t + 128] - b, 0.0)
                g_own[r, pl.ds(2 * n + t, 1), :] = jnp.sum(part, axis=0, keepdims=True)
        return 0

    def to_sib(p):
        go(g_own.at[1 - c, pl.ds(8 * p, 8)], g_sib.at[pl.ds(8 * p, 8)], gs_s.at[p], gs_r.at[p], sib, col)

    def to_levels(p):
        part = pl.ds(8 * p, 8)
        arrived(g_sib.at[part], gs_r.at[p])
        g_all[0, part] = g_own[c, part] + g_sib[part]
        for d in (8, 7, 9, 6, 10, 5, 11, 4, 12, 3, 13, 2, 14, 1, 15):
            go(g_all.at[0, part], g_all.at[d, part], gz_s.at[p, d - 1], gz_r.at[p, d - 1],
               ((z + d) % LEVELS) * 2 + c, col)

    lax.fori_loop(0, 4, second_half, 0)
    to_sib(0)
    lax.fori_loop(4, 6, second_half, 0)
    to_levels(0)
    lax.fori_loop(6, 8, second_half, 0)
    to_sib(1)
    to_levels(1)
    for p in range(2):
        part = pl.ds(8 * p, 8)
        for d in range(1, LEVELS):
            arrived(g_all.at[d, part], gz_r.at[p, d - 1])
    total = g_all[0]
    for d in range(1, LEVELS):
        total = total + g_all[d]
    g_sum[c] = total * (1.0 / 32768.0)
    go(g_sum.at[c], g_sum.at[c], gf_s, gf_r, sib, col)
    arrived(g_sum.at[1 - c], gf_r)
    for r in range(2):
        for t in range(16):
            gains_out[pl.ds(r, 1), pl.ds(128 * t, 128)] = g_sum[r, pl.ds(t, 1), :]
    for copy in pending:
        copy.wait_send()


def on_device(example_sketch, candidate_sketch, best_start, chosen):
    dma = pltpu.SemaphoreType.DMA
    vmem = pltpu.VMEM
    examples, candidates = example_sketch.shape[1], candidate_sketch.shape[1]
    widths = LEVELS * GROUP
    best, gains = pl.pallas_call(
        kernel,
        out_shape=(
            jax.ShapeDtypeStruct((8, 128), F32),
            jax.ShapeDtypeStruct((2, candidates), F32),
        ),
        in_specs=[
            pl.BlockSpec(memory_space=pl.ANY),
            pl.BlockSpec(memory_space=pl.ANY),
            pl.BlockSpec(memory_space=pltpu.VMEM),
            pl.BlockSpec(memory_space=pltpu.SMEM),
        ],
        out_specs=(pl.BlockSpec(memory_space=pltpu.VMEM), pl.BlockSpec(memory_space=pltpu.VMEM)),
        scratch_shapes=[
            vmem((widths, candidates), F32),
            vmem((widths, candidates), BF16),
            vmem((widths, candidates), BF16),
            vmem((8, candidates), F32),
            vmem((widths, examples), F32),
            vmem((examples, widths), BF16),
            vmem((examples, widths), BF16),
            vmem((examples, candidates), F32),
            vmem((2, examples, 128), F32),
            vmem((8, 8, 128), F32),
            vmem((LEVELS, 8, 128), F32),
            vmem((widths, 256), BF16),
            vmem((widths, 256), BF16),
            vmem((2, 16, 128), F32),
            vmem((16, 128), F32),
            vmem((LEVELS, 16, 128), F32),
            vmem((2, 16, 128), F32),
            dma((2,)),
            dma((8, 2, PIECES)),
            dma((8, 2, PIECES)),
            dma((10,)),
            dma((10,)),
            dma((2, 3)),
            dma((2, 3)),
            dma((2, 4, 3)),
            dma((2, 4, 3)),
            dma((2, 3)),
            dma((2, 3)),
            dma((2, 4)),
            dma((2, 4)),
            dma((2,)),
            dma((2,)),
            dma((2,)),
            dma((2,)),
            dma((2, 15)),
            dma((2, 15)),
            dma,
            dma,
        ],
        compiler_params=pltpu.CompilerParams(
            collective_id=0, has_side_effects=True, vmem_limit_bytes=48 * 1024 * 1024
        ),
        cost_estimate=pl.CostEstimate(flops=6 * 512 * 1024 * 2048, bytes_accessed=300000, transcendentals=4096),
    )(example_sketch, candidate_sketch, best_start.reshape(8, 128), chosen)
    return best.reshape(examples), gains


def solution(mesh):
    return jax.shard_map(
        on_device,
        mesh=mesh,
        in_specs=(P("col", "row"), P("row", "col"), P("row"), P()),
        out_specs=(P("row"), P(None, "col")),
        check_vma=False,
    )
```

time: 188 us -> 80.7 us (0.43)
  Pallas kernels: 0 us -> 75.5 us
  waiting for transfers between devices: 65.9 us -> 0 us
  blocking collectives: 62.3 us -> 0 us
  between operations: 19.4 us -> 0.65 us
  matrix products: 16.3 us -> 0 us
  other arithmetic: 8.58 us -> 0 us
  starting transfers between devices: 7.62 us -> 0 us
  local copies, waits for them, and re-layouts: 7.25 us -> 4.34 us
    pallas_call x0 -> x1, Pallas kernels: none -> 75.5 us  [on_device(): pl.pallas_call(kernel, out_shape=(jax.ShapeDtypeStruct((8, 128), F32), ja...]
    all_gather x1 -> x0, waiting for transfers between devices: 46.6 us -> none  [on_device(): cand_full = lax.all_gather(candidate_sketch, 'row', axis=0, tiled=True)]
    all_to_all x1 -> x0, blocking collectives: 45.3 us -> none  [from_everyone(): return lax.all_to_all(copies, axis, split_axis=0, concat_axis=0, tiled=True)]
    all_to_all x1 -> x0, waiting for transfers between devices: 18.6 us -> none  [from_everyone(): return lax.all_to_all(copies, axis, split_axis=0, concat_axis=0, tiled=True)]
    psum x2 -> x0, blocking collectives: 17 us -> none  [broadcast_by_axis(): array = lax.psum(array, axis)]
    dot_general x1 -> x0, matrix products: 16.3 us -> none  [on_device(): lax.dot_general(examples_full, cand_full, (((0,), (0,)), ((), ())), preci...]
    all_to_all x1 -> x0, starting transfers between devices: 7.58 us -> none  [from_everyone(): return lax.all_to_all(copies, axis, split_axis=0, concat_axis=0, tiled=True)]
    reduce_sum x4 -> x0, other arithmetic: 7.29 us -> none  [the longest x1 4.39 us: on_device(): local_gain = jnp.sum(jnp.maximum(similar - best[:, None], 0.0), axis=0)]
  transfers between devices with their start and end apart: 2 -> 0, of which waited for: 2 -> 0; matrix products, arithmetic and copies ran while one was open for 2% -> 0% of each run, Pallas kernels for 0% -> 0%
where the time goes in v1:
time: 80.7 us; the launch traced here: 80.5 us
  Pallas kernels  75.5 us (94%)
  local copies, waits for them, and re-layouts  4.34 us (5%)
    pallas_call x1, Pallas kernels, on_device(): pl.pallas_call(kernel, out_shape=(jax.ShapeDtypeStruct((8, 128), F32), ja...  75.5 us
    unnamed x10, local copies, waits for them, and re-layouts  4.34 us

profile of v1, /device:TPU:1, one launch (start us, length us, event | category | flops | bytes accessed | tf_op | source)
XLA Modules:
  0.0 80.5 jit_solution(5383072308701144793)
XLA Ops:
  0.6 0.0 copy-start.3
  0.6 0.6 copy-done.3
  1.3 0.0 copy-start
  1.3 0.9 %copy-done = f32[32,1024]{1,0:T(8,128)S(1)} copy-done((f32[32,1024]{1,0:T(8,128)S(1)}, f32[32,1024]{1,0:T(8,128)}, u32[]{:S(2)}) %copy-start) | copy-done | bytes 131096
  2.2 0.0 copy-start.1
  2.2 0.9 %copy-done.1 = f32[16,2048]{1,0:T(8,128)S(1)} copy-done((f32[16,2048]{1,0:T(8,128)S(1)}, f32[16,2048]{1,0:T(8,128)}, u32[]{:S(2)}) %copy-start.1) | copy-done | bytes 131096
  3.1 0.0 copy-start.2
  3.1 0.7 copy-done.2
  3.8 75.5 %shard_map.59 = (f32[8,128]{1,0:T(8,128)S(1)}, f32[2,2048]{1,0:T(2,128)S(1)}) custom-call(f32[32,1024]{1,0:T(8,128)S(1)} %copy-done, f32[16,2048]{1,0:T(8,128)S(1)} %copy-done.1, f32[8,128]{1,0:T(8,128)S(1)} %bitcast.3, s32[2]{0:T(128)S(1)} %copy-done.3), custom_call_target="tpu_custom_call" | custom-call | flops 6442450944 | bytes 300000 | tf_op jit(solution)/shard_map/pallas_call | solution.py:333
  79.3 0.6 copy.8
  79.9 0.6 copy.9
Async XLA Ops:
  0.6 0.7 copy-start.3
  1.3 0.9 %copy-start = (f32[32,1024]{1,0:T(8,128)S(1)}, f32[32,1024]{1,0:T(8,128)}, u32[]{:S(2)}) copy-start(f32[32,1024]{1,0:T(8,128)} %ex_hbm.1) | copy-start | bytes 393220
  2.2 0.9 %copy-start.1 = (f32[16,2048]{1,0:T(8,128)S(1)}, f32[16,2048]{1,0:T(8,128)}, u32[]{:S(2)}) copy-start(f32[16,2048]{1,0:T(8,128)} %cand_hbm.1) | copy-start | bytes 393220
  3.1 0.7 copy-start.2

commit v2 on v0

v2 whole, which is shorter than its diff:
```python
import functools

import jax
import jax.numpy as jnp
from jax import lax
from jax.experimental import pallas as pl
from jax.experimental.pallas import tpu as pltpu
from jax.sharding import PartitionSpec as P

EPS = 1e-06
LEVELS = 16
GROUP = 32
PIECES = 4
TILE = 256
F32, BF16 = jnp.float32, jnp.bfloat16


def remote(src, dst, send, recv, row, col):
    return pltpu.make_async_remote_copy(
        src_ref=src,
        dst_ref=dst,
        send_sem=send,
        recv_sem=recv,
        device_id={"row": row, "col": col},
        device_id_type=pl.DeviceIdType.MESH,
    )


def slot_rows(slot):
    return pl.ds((slot % LEVELS) * GROUP, GROUP)


def kernel(
    ex_hbm, cand_hbm, best_hbm, chosen_hbm, best_out, gains_out,
    cand, c_hi, c_lo, c_sq, ex, e_hi, e_lo, acc, best_rep, best_in, chosen, ch_part, ch, ch_hi, ch_lo,
    g_own, g_sib, g_all, g_sum,
    loc_sem, ring_s, ring_r, sib_s, sib_r, p1_s, p1_r, p2_s, p2_r, wave,
    cx_s, cx_r, z1_s, z1_r, z2_s, z2_r, gs_s, gs_r, gz_s, gz_r, gf_s, gf_r,
):
    row, col = lax.axis_index("row"), lax.axis_index("col")
    z, c, y, x = row // 2, row % 2, col // 4, col % 4

    def in_x(d):
        return y * 4 + (x + d) % 4

    def in_y(d):
        return ((y + d) % 4) * 4 + x

    def in_z(d):
        return ((z + d + LEVELS) % LEVELS) * 2 + c

    above, below = ((z + 1) % LEVELS) * 2, ((z + LEVELS - 1) % LEVELS) * 2
    sib = z * 2 + 1 - c
    onward = jnp.where(c == 0, above, below + 1)
    pending = []

    def go(*args):
        copy = remote(*args)
        copy.start()
        pending.append(copy)

    def arrived(view, sem):
        remote(view, view, loc_sem.at[0], sem, sib, col).wait_recv()

    barrier = pltpu.get_barrier_semaphore()
    near = [(r, col) for r in (above, above + 1, below, below + 1, sib)]
    near += [(row, t) for d in (1, 2, 3) for t in (in_x(d), in_y(d))]
    for r, t in near:
        pl.semaphore_signal(
            barrier, inc=1, device_id={"row": r, "col": t}, device_id_type=pl.DeviceIdType.MESH
        )

    mine = pl.ds(pl.multiple_of(4 * GROUP + c * 16, 16), 16)

    def ex_view(t, half, rows=16, skip=0):
        slot = (t - z + 4 + LEVELS) % LEVELS
        return ex.at[pl.ds(pl.multiple_of(slot * GROUP + 16 * half + skip, 8), rows)]

    copies = [
        pltpu.make_async_copy(cand_hbm, cand.at[mine], loc_sem.at[0]),
        pltpu.make_async_copy(chosen_hbm, chosen, loc_sem.at[1]),
        pltpu.make_async_copy(ex_hbm, ex_view(col, 0, 32), loc_sem.at[2]),
        pltpu.make_async_copy(best_hbm, best_in, loc_sem.at[3]),
    ]
    for copy in copies:
        copy.start()
    copies[0].wait()
    copies[1].wait()

    lane = lax.broadcasted_iota(jnp.int32, (128, 128), 1)
    sub = lax.broadcasted_iota(jnp.int32, (128, 128), 0)

    block = cand[mine, :]
    wide = lax.broadcasted_iota(jnp.int32, block.shape, 1)
    tile = jnp.zeros((8, 128), F32)
    for r in range(2):
        place = chosen[r] - col * block.shape[1]
        value = jnp.sum(jnp.where(wide == place, block, 0.0), axis=1, keepdims=True)
        line = jnp.sum(
            jnp.where(lane[:16] == sub[:16] + (GROUP * (z % 4) + 16 * c), value, 0.0), axis=0, keepdims=True
        )
        tile = tile + jnp.where(sub[:8] == r, line, 0.0)
    ch_part[0] = tile
    copies[2].wait()
    copies[3].wait()
    pl.semaphore_wait(barrier, len(near))

    def wave_send(i):
        for k, r in enumerate((in_z(1), in_z(-1))):
            pl.semaphore_signal(
                wave.at[i, k], inc=1, device_id={"row": r, "col": col}, device_id_type=pl.DeviceIdType.MESH
            )

    def wave_wait(i):
        pl.semaphore_wait(wave.at[i, 0], 1)
        pl.semaphore_wait(wave.at[i, 1], 1)

    wave_send(0)

    width = cand.shape[1] * 2 // PIECES

    def piece(first_row, half, k):
        start = pl.multiple_of(first_row + 8 * half, 8)
        return cand.at[pl.ds(start, 8), pl.ds((k // 2) * width, width)]

    for k in range(PIECES):
        src = piece(4 * GROUP + c * 16, k % 2, k)
        go(src, piece(3 * GROUP + c * 16, k % 2, k), ring_s.at[0, 0, k], ring_r.at[0, c, k], above, col)
        go(src, piece(5 * GROUP + c * 16, k % 2, k), ring_s.at[0, 1, k], ring_r.at[0, c, k], below + 1, col)
    go(cand.at[mine], cand.at[mine], sib_s.at[0, 0, 0], sib_r.at[0], sib, col)
    two = pl.ds(0, 2)
    for j in range(3):
        go(ch_part.at[0, two], ch_part.at[2 + j, two], cx_s.at[0, j], cx_r.at[0, j], row, in_x(j + 1))

    lines = ((in_x, in_y), (in_y, in_x))

    def spread(half, phase, i, view):
        s, r = (p1_s, p1_r) if phase == 0 else (p2_s, p2_r)
        for k, d in enumerate((1, 3)):
            go(view, view, s.at[half, i, k], r.at[half, i, k], row, lines[half][phase](d))

    def relay(half, phase, i, k, owner):
        s, r = (p1_s, p1_r) if phase == 0 else (p2_s, p2_r)
        arrived(ex_view(owner, half), r.at[half, i, k])
        view = ex_view(owner, half, 8, 8 * k)
        go(view, view, s.at[half, i, 2 + k], r.at[half, i, 2 + k], row, lines[half][phase]((1, 3)[k]))

    def opposite(half, phase, i):
        r = p1_r if phase == 0 else p2_r
        arrived(ex.at[pl.ds(0, 8)], r.at[half, i, 2])
        arrived(ex.at[pl.ds(0, 8)], r.at[half, i, 3])

    def first(half, d):
        return lines[half][0](d)

    def second(half, d1, d2):
        xx, yy = (d1, d2) if half == 0 else (d2, d1)
        return ((y + yy) % 4) * 4 + (x + xx) % 4

    for half in range(2):
        spread(half, 0, 0, ex_view(col, half))
    for half in range(2):
        spread(half, 1, 0, ex_view(col, half))

    plan = {}

    def at(h, i, *fns):
        plan.setdefault((h, i), []).extend(fns)

    def call(fn, *args):
        return functools.partial(fn, *args)

    def phase_one(half, k):
        d = (3, 1)[k]
        relay(half, 0, 0, k, first(half, d))
        spread(half, 1, d, ex_view(first(half, d), half))

    def phase_one_far(half):
        opposite(half, 0, 0)
        spread(half, 1, 2, ex_view(first(half, 2), half))

    def phase_two(half, d, k):
        relay(half, 1, d, k, second(half, d, (3, 1)[k]))

    def from_sib(h):
        arrived(cand.at[pl.ds(0, 16 if h in (0, 8) else GROUP)], sib_r.at[h])

    def prepare(slot):
        v = cand[slot_rows(slot), :]
        hi = v.astype(BF16)
        c_hi[slot_rows(slot), :] = hi
        c_lo[slot_rows(slot), :] = (v - hi.astype(F32)).astype(BF16)
        sq = v * v
        c_sq[...] += sq[0:8] + sq[8:16] + sq[16:24] + sq[24:32]

    def chosen_y():
        for j in range(3):
            arrived(ch_part.at[2 + j, two], cx_r.at[0, j])
        ch_part[1, two] = ch_part[0, two] + ch_part[2, two] + ch_part[3, two] + ch_part[4, two]
        for j in range(3):
            go(ch_part.at[1, two], ch_part.at[5 + j, two], cx_s.at[1, j], cx_r.at[1, j], row, in_y(j + 1))

    def chosen_sib():
        for j in range(3):
            arrived(ch_part.at[5 + j, two], cx_r.at[1, j])
        ch_part[8, two] = ch_part[1, two] + ch_part[5, two] + ch_part[6, two] + ch_part[7, two]
        go(ch_part.at[8, two], ch_part.at[9, two], cx_s.at[2, 0], cx_r.at[2, 0], sib, col)

    def chosen_near():
        arrived(ch_part.at[9, two], cx_r.at[2, 0])
        ch[4, two] = ch_part[8, two] + ch_part[9, two]
        for d in range(1, 5):
            go(ch.at[4, two], ch.at[4 - d, two], z1_s.at[0, d - 1], z1_r.at[0, d - 1], in_z(d), col)
            go(ch.at[4, two], ch.at[4 + d, two], z1_s.at[1, d - 1], z1_r.at[1, d - 1], in_z(-d), col)

    def chosen_far():
        for d in range(1, 5):
            arrived(ch.at[0, two], z1_r.at[0, d - 1])
            arrived(ch.at[0, two], z1_r.at[1, d - 1])
        go(ch.at[pl.ds(0, 4), two], ch.at[pl.ds(12, 4), two], z2_s.at[0], z2_r.at[0], in_z(4), col)
        go(ch.at[pl.ds(5, 3), two], ch.at[pl.ds(9, 3), two], z2_s.at[1], z2_r.at[1], in_z(-4), col)

    held = {"e_sq": jnp.zeros((8, ex.shape[1]), F32), "ch_sq": [jnp.zeros((1, 128), F32)] * 2}

    def square(part):
        total = held["e_sq"]
        for i in range(32 * part, 32 * part + 32):
            v = ex[pl.ds(8 * i, 8), :]
            total = total + v * v
        held["e_sq"] = total
        if part == 1:
            scale = jnp.sqrt(jnp.float32(LEVELS * GROUP))
            held["factor"] = scale / jnp.sqrt(jnp.sum(total, axis=0, keepdims=True) + EPS)

    def turn(i, q):
        v = ex[pl.ds(128 * q, 128), pl.ds(128 * i, 128)] * held["factor"][:, 128 * i : 128 * (i + 1)]
        v = v.T
        hi = v.astype(BF16)
        e_hi[pl.ds(128 * i, 128), pl.ds(128 * q, 128)] = hi
        e_lo[pl.ds(128 * i, 128), pl.ds(128 * q, 128)] = (v - hi.astype(F32)).astype(BF16)

    def chosen_wide(q):
        four = ch[4 * q, two] + ch[4 * q + 1, two] + ch[4 * q + 2, two] + ch[4 * q + 3, two]
        for r in range(2):
            v = jnp.broadcast_to(four[r : r + 1, :], (128, 128)).T
            held["ch_sq"] = [
                s + jnp.sum(v * v, axis=0, keepdims=True) if k == r else s for k, s in enumerate(held["ch_sq"])
            ]
            hi = v.astype(BF16)
            lo = (v - hi.astype(F32)).astype(BF16)
            for b in range(4):
                to = pl.ds(pl.multiple_of(((b - z + LEVELS) % 4 + 4 * q) * GROUP, GROUP), GROUP)
                ch_hi[to, pl.ds(128 * r, 128)] = hi[32 * b : 32 * b + 32]
                ch_lo[to, pl.ds(128 * r, 128)] = lo[32 * b : 32 * b + 32]

    def chosen_come():
        arrived(ch.at[pl.ds(0, 4), two], z2_r.at[0])
        arrived(ch.at[pl.ds(0, 3), two], z2_r.at[1])

    dot = functools.partial(jnp.dot, preferred_element_type=F32)

    def pick(i):
        rows = pl.ds(i * 256, 256)
        hi, lo = e_hi[rows, :], e_lo[rows, :]
        d = dot(hi, ch_hi[...]) + dot(lo, ch_hi[...]) + dot(hi, ch_lo[...])
        b = best_rep[0, rows, :]
        for r in range(2):
            b = jnp.maximum(b, d[:, 128 * r : 128 * r + 128] / jnp.sqrt(held["ch_sq"][r] + EPS))
            best_rep[r, rows, :] = b
        for k in range(2):
            best_out[pl.ds(2 * i + k, 1), :] = jnp.sum(
                jnp.where(lane == sub, b[128 * k : 128 * k + 128], 0.0), axis=0, keepdims=True
            )

    def first_half(n, m):
        cols, rows = pl.ds(n * TILE, TILE), pl.ds(m * 512, 512)
        hi, lo = c_hi[pl.ds(0, 256), cols], c_lo[pl.ds(0, 256), cols]
        a_hi, a_lo = e_hi[rows, pl.ds(0, 256)], e_lo[rows, pl.ds(0, 256)]
        acc[rows, cols] = dot(a_hi, hi) + dot(a_lo, hi) + dot(a_hi, lo)

    at(1, 3, call(wave_wait, 2), chosen_y)
    at(2, 7, chosen_sib)
    at(3, 3, chosen_near)
    at(5, 4, chosen_far)
    at(7, 2, chosen_come, call(chosen_wide, 0))
    at(7, 3, call(chosen_wide, 1))
    at(7, 4, call(chosen_wide, 2))
    at(7, 5, call(chosen_wide, 3))
    for n, (half, k) in enumerate(((0, 0), (0, 1), (1, 0), (1, 1))):
        at(1, (1, 2, 4, 5)[n], call(phase_one, half, k))
        at(2, n, call(phase_two, half, 0, k))
        at(3, 2 * (n % 2) + 1, call(phase_two, half, 1, k))
        at(3, 2 * (n % 2) + 4, call(phase_two, half, 3, k))
        at(4, n, call(phase_two, half, 2, k))
    at(2, 5, call(phase_one_far, 0))
    at(2, 6, call(phase_one_far, 1))
    for half in range(2):
        for d in range(4):
            at(5, 0, call(opposite, half, 1, d))
    at(5, 1, call(square, 0))
    at(5, 2, call(square, 1))
    work = [call(turn, i, q) for q in range(2) for i in range(8)]
    for i, fn in enumerate(work):
        at(5, 3 + i // 4, fn)
    work = [call(turn, i, q) for q in range(2, 4) for i in range(8)]
    for i, fn in enumerate(work):
        at(6, 6 + i // 8, fn)
    for h in range(1, 7):
        at(h + 1, 3, call(from_sib, h))
        at(h + 1, 4, call(prepare, (4 - h) % LEVELS))
        at(h + 1, 5, call(prepare, 4 + h))
    halves = [(n, m) for n in range(8) for m in range(2)]
    for i, (n, m) in enumerate(halves[:6]):
        at(6, i, call(first_half, n, m))
    for i, (n, m) in enumerate(halves[6:14]):
        at(7, i, call(first_half, n, m))
    for i, (n, m) in enumerate(halves[14:]):
        at(8, i, call(first_half, n, m))
    for i in range(4):
        at(7, 6 + i // 2, call(pick, i))

    c_sq[...] = jnp.zeros_like(c_sq)
    for i in range(8):
        best_rep[0, pl.ds(128 * i, 128), :] = jnp.broadcast_to(best_in[pl.ds(i, 1), :], (128, 128)).T
    wave_wait(0)
    wave_send(1)
    from_sib(0)
    prepare(4)
    wave_wait(1)
    wave_send(2)

    for h in range(1, 9):
        base = jnp.where(c == 0, ((4 - h) % LEVELS) * GROUP, ((4 + h) % LEVELS) * GROUP)
        after = jnp.where(c == 0, ((3 - h) % LEVELS) * GROUP, ((5 + h) % LEVELS) * GROUP)
        event = 0
        for k in range(PIECES):
            for o in range(2):
                far = k % 2 == 0
                if h == 8 and not far:
                    continue
                half = (k % 2 + c) % 2
                view = piece(base + o * 16, half, k)
                kk = (k // 2) * 2 + half if h == 1 else k
                arrived(view, ring_r.at[h - 1, o, kk])
                if h < 7 or (far and h < 8):
                    go(view, piece(after + o * 16, half, k), ring_s.at[h, o, k], ring_r.at[h, o, k], onward, col)
                go(view, view, sib_s.at[h, o, k], sib_r.at[h], sib, col)
                for fn in plan.pop((h, event), ()):
                    fn()
                event += 1
    assert not plan
    from_sib(7)
    prepare(13)
    prepare(11)
    from_sib(8)
    prepare(12)

    def second_half(n, _):
        cols = pl.ds(pl.multiple_of(n * TILE, TILE), TILE)
        hi, lo = c_hi[pl.ds(256, 256), cols], c_lo[pl.ds(256, 256), cols]
        a_hi, a_lo = e_hi[:, pl.ds(256, 256)], e_lo[:, pl.ds(256, 256)]
        d = acc[:, cols] + (dot(a_hi, hi) + dot(a_lo, hi) + dot(a_hi, lo))
        norm = jnp.sqrt(jnp.sum(c_sq[:, cols], axis=0, keepdims=True) + EPS)
        sim = d * (1.0 / norm)
        for r in range(2):
            b = best_rep[r]
            for t in range(2):
                part = jnp.maximum(sim[:, 128 * t : 128 * t + 128] - b, 0.0)
                g_own[r, pl.ds(2 * n + t, 1), :] = jnp.sum(part, axis=0, keepdims=True)
        return 0

    def rows_of(p):
        return pl.ds(4 * p, 4)

    def to_sib(p):
        go(g_own.at[1 - c, rows_of(p)], g_sib.at[rows_of(p)], gs_s.at[p], gs_r.at[p], sib, col)

    def to_levels(p):
        part = rows_of(p)
        arrived(g_sib.at[part], gs_r.at[p])
        g_all[0, part] = g_own[c, part] + g_sib[part]
        for d in (8, 7, 9, 6, 10, 5, 11, 4, 12, 3, 13, 2, 14, 1, 15):
            go(g_all.at[0, part], g_all.at[d, part], gz_s.at[p, d - 1], gz_r.at[p, d - 1], in_z(d), col)

    for p in range(4):
        lax.fori_loop(2 * p, 2 * p + 2, second_half, 0)
        to_sib(p)
        if p > 0:
            to_levels(p - 1)
    to_levels(3)
    for p in range(4):
        for d in range(1, LEVELS):
            arrived(g_all.at[d, rows_of(p)], gz_r.at[p, d - 1])
    total = g_all[0]
    for d in range(1, LEVELS):
        total = total + g_all[d]
    g_sum[c] = total * (1.0 / 32768.0)
    go(g_sum.at[c], g_sum.at[c], gf_s, gf_r, sib, col)
    arrived(g_sum.at[1 - c], gf_r)
    for r in range(2):
        for t in range(16):
            gains_out[pl.ds(r, 1), pl.ds(128 * t, 128)] = g_sum[r, pl.ds(t, 1), :]
    for copy in pending:
        copy.wait_send()


def on_device(example_sketch, candidate_sketch, best_start, chosen):
    dma = pltpu.SemaphoreType.DMA
    vmem = pltpu.VMEM
    examples, candidates = example_sketch.shape[1], candidate_sketch.shape[1]
    widths = LEVELS * GROUP
    best, gains = pl.pallas_call(
        kernel,
        out_shape=(
            jax.ShapeDtypeStruct((8, 128), F32),
            jax.ShapeDtypeStruct((2, candidates), F32),
        ),
        in_specs=[
            pl.BlockSpec(memory_space=pltpu.HBM),
            pl.BlockSpec(memory_space=pltpu.HBM),
            pl.BlockSpec(memory_space=pltpu.HBM),
            pl.BlockSpec(memory_space=pltpu.HBM),
        ],
        out_specs=(pl.BlockSpec(memory_space=pltpu.VMEM), pl.BlockSpec(memory_space=pltpu.VMEM)),
        scratch_shapes=[
            vmem((widths, candidates), F32),
            vmem((widths, candidates), BF16),
            vmem((widths, candidates), BF16),
            vmem((8, candidates), F32),
            vmem((widths, examples), F32),
            vmem((examples, widths), BF16),
            vmem((examples, widths), BF16),
            vmem((examples, candidates), F32),
            vmem((2, examples, 128), F32),
            vmem((8, 128), F32),
            pltpu.SMEM((2,), jnp.int32),
            vmem((10, 8, 128), F32),
            vmem((LEVELS, 8, 128), F32),
            vmem((widths, 256), BF16),
            vmem((widths, 256), BF16),
            vmem((2, 16, 128), F32),
            vmem((16, 128), F32),
            vmem((LEVELS, 16, 128), F32),
            vmem((2, 16, 128), F32),
            dma((4,)),
            dma((8, 2, PIECES)),
            dma((8, 2, PIECES)),
            dma((9, 2, PIECES)),
            dma((9,)),
            dma((2, 1, 4)),
            dma((2, 1, 4)),
            dma((2, 4, 4)),
            dma((2, 4, 4)),
            pltpu.SemaphoreType.REGULAR((3, 2)),
            dma((3, 3)),
            dma((3, 3)),
            dma((2, 4)),
            dma((2, 4)),
            dma((2,)),
            dma((2,)),
            dma((4,)),
            dma((4,)),
            dma((4, 15)),
            dma((4, 15)),
            dma,
            dma,
        ],
        compiler_params=pltpu.CompilerParams(
            collective_id=0, has_side_effects=True, vmem_limit_bytes=60 * 1024 * 1024
        ),
        cost_estimate=pl.CostEstimate(flops=6 * 512 * 1024 * 2048, bytes_accessed=300000, transcendentals=4096),
    )(example_sketch, candidate_sketch, best_start.reshape(8, 128), chosen)
    return best.reshape(examples), gains


def solution(mesh):
    return jax.shard_map(
        on_device,
        mesh=mesh,
        in_specs=(P("col", "row"), P("row", "col"), P("row"), P()),
        out_specs=(P("row"), P(None, "col")),
        check_vma=False,
    )
```

time: 188 us -> 70.2 us (0.37)
  Pallas kernels: 0 us -> 66.7 us
  waiting for transfers between devices: 65.9 us -> 0 us
  blocking collectives: 62.3 us -> 0 us
  between operations: 19.4 us -> 0.65 us
  matrix products: 16.3 us -> 0 us
  other arithmetic: 8.58 us -> 0 us
  starting transfers between devices: 7.62 us -> 0 us
  local copies, waits for them, and re-layouts: 7.25 us -> 2.59 us
    pallas_call x0 -> x1, Pallas kernels: none -> 66.7 us  [on_device(): pl.pallas_call(kernel, out_shape=(jax.ShapeDtypeStruct((8, 128), F32), ja...]
    all_gather x1 -> x0, waiting for transfers between devices: 46.6 us -> none  [on_device(): cand_full = lax.all_gather(candidate_sketch, 'row', axis=0, tiled=True)]
    all_to_all x1 -> x0, blocking collectives: 45.3 us -> none  [from_everyone(): return lax.all_to_all(copies, axis, split_axis=0, concat_axis=0, tiled=True)]
    all_to_all x1 -> x0, waiting for transfers between devices: 18.6 us -> none  [from_everyone(): return lax.all_to_all(copies, axis, split_axis=0, concat_axis=0, tiled=True)]
    psum x2 -> x0, blocking collectives: 17 us -> none  [broadcast_by_axis(): array = lax.psum(array, axis)]
    dot_general x1 -> x0, matrix products: 16.3 us -> none  [on_device(): lax.dot_general(examples_full, cand_full, (((0,), (0,)), ((), ())), preci...]
    all_to_all x1 -> x0, starting transfers between devices: 7.58 us -> none  [from_everyone(): return lax.all_to_all(copies, axis, split_axis=0, concat_axis=0, tiled=True)]
    reduce_sum x4 -> x0, other arithmetic: 7.29 us -> none  [the longest x1 4.39 us: on_device(): local_gain = jnp.sum(jnp.maximum(similar - best[:, None], 0.0), axis=0)]
  transfers between devices with their start and end apart: 2 -> 0, of which waited for: 2 -> 0; matrix products, arithmetic and copies ran while one was open for 2% -> 0% of each run, Pallas kernels for 0% -> 0%
where the time goes in v2:
time: 70.2 us; the launch traced here: 70 us
  Pallas kernels  66.7 us (95%)
  local copies, waits for them, and re-layouts  2.59 us (4%)
    pallas_call x1, Pallas kernels, on_device(): pl.pallas_call(kernel, out_shape=(jax.ShapeDtypeStruct((8, 128), F32), ja...  66.7 us
    unnamed x4, local copies, waits for them, and re-layouts  2.59 us

profile of v2, /device:TPU:1, one launch (start us, length us, event | category | flops | bytes accessed | tf_op | source)
XLA Modules:
  0.0 70.0 jit_solution(17125414694531777758)
XLA Ops:
  0.6 66.7 %shard_map.59 = (f32[8,128]{1,0:T(8,128)}, f32[2,2048]{1,0:T(2,128)}) custom-call(f32[32,1024]{1,0:T(8,128)} %ex_hbm.1, f32[16,2048]{1,0:T(8,128)} %cand_hbm.1, f32[8,128]{1,0:T(8,128)} %bitcast.3, s32[2]{0:T(128)} %chosen_hbm.1), custom_call_target="tpu_custom_call" | custom-call | flops 6442450944 | bytes 300000 | tf_op jit(solution)/shard_map/pallas_call | solution.py:412
  67.4 0.0 copy-start
  67.4 0.7 copy-done
  68.0 0.6 copy.8
  68.6 1.3 %copy.9 = f32[2,2048]{1,0:T(2,128)} copy(f32[2,2048]{1,0:T(2,128)} %get-tuple-element.9) | data formatting | bytes 32768
Async XLA Ops:
  67.4 0.7 copy-start

commit v3 on v2

--- a/solution.py
+++ b/solution.py
@@ -52,12 +52,13 @@
     above, below = ((z + 1) % LEVELS) * 2, ((z + LEVELS - 1) % LEVELS) * 2
     sib = z * 2 + 1 - c
     onward = jnp.where(c == 0, above, below + 1)
-    pending = []
+    sent = []
 
     def go(*args):
-        copy = remote(*args)
-        copy.start()
-        pending.append(copy)
+        remote(*args).start()
+
+    def left(view, sem):
+        sent.append(remote(view, view, sem, loc_sem.at[0], sib, col))
 
     def arrived(view, sem):
         remote(view, view, loc_sem.at[0], sem, sib, col).wait_recv()
@@ -125,25 +126,29 @@
 
     for k in range(PIECES):
         src = piece(4 * GROUP + c * 16, k % 2, k)
-        go(src, piece(3 * GROUP + c * 16, k % 2, k), ring_s.at[0, 0, k], ring_r.at[0, c, k], above, col)
-        go(src, piece(5 * GROUP + c * 16, k % 2, k), ring_s.at[0, 1, k], ring_r.at[0, c, k], below + 1, col)
-    go(cand.at[mine], cand.at[mine], sib_s.at[0, 0, 0], sib_r.at[0], sib, col)
+        go(src, piece(3 * GROUP + c * 16, k % 2, k), ring_s.at[0], ring_r.at[0, c, k], above, col)
+        go(src, piece(5 * GROUP + c * 16, k % 2, k), ring_s.at[0], ring_r.at[0, c, k], below + 1, col)
+    go(cand.at[mine], cand.at[mine], sib_s.at[0], sib_r.at[0], sib, col)
+    left(cand.at[pl.ds(0, 32)], ring_s.at[0])
+    left(cand.at[pl.ds(0, 16)], sib_s.at[0])
     two = pl.ds(0, 2)
     for j in range(3):
-        go(ch_part.at[0, two], ch_part.at[2 + j, two], cx_s.at[0, j], cx_r.at[0, j], row, in_x(j + 1))
+        go(ch_part.at[0, two], ch_part.at[2 + j, two], cx_s.at[0], cx_r.at[0, j], row, in_x(j + 1))
+    left(ch.at[pl.ds(0, 3), two], cx_s.at[0])
 
     lines = ((in_x, in_y), (in_y, in_x))
 
     def spread(half, phase, i, view):
         s, r = (p1_s, p1_r) if phase == 0 else (p2_s, p2_r)
         for k, d in enumerate((1, 3)):
-            go(view, view, s.at[half, i, k], r.at[half, i, k], row, lines[half][phase](d))
+            go(view, view, s.at[half, i], r.at[half, i, k], row, lines[half][phase](d))
+        left(ex.at[pl.ds(0, 48)], s.at[half, i])
 
     def relay(half, phase, i, k, owner):
         s, r = (p1_s, p1_r) if phase == 0 else (p2_s, p2_r)
         arrived(ex_view(owner, half), r.at[half, i, k])
         view = ex_view(owner, half, 8, 8 * k)
-        go(view, view, s.at[half, i, 2 + k], r.at[half, i, 2 + k], row, lines[half][phase]((1, 3)[k]))
+        go(view, view, s.at[half, i], r.at[half, i, 2 + k], row, lines[half][phase]((1, 3)[k]))
 
     def opposite(half, phase, i):
         r = p1_r if phase == 0 else p2_r
@@ -198,27 +203,32 @@
             arrived(ch_part.at[2 + j, two], cx_r.at[0, j])
         ch_part[1, two] = ch_part[0, two] + ch_part[2, two] + ch_part[3, two] + ch_part[4, two]
         for j in range(3):
-            go(ch_part.at[1, two], ch_part.at[5 + j, two], cx_s.at[1, j], cx_r.at[1, j], row, in_y(j + 1))
+            go(ch_part.at[1, two], ch_part.at[5 + j, two], cx_s.at[1], cx_r.at[1, j], row, in_y(j + 1))
+        left(ch.at[pl.ds(0, 3), two], cx_s.at[1])
 
     def chosen_sib():
         for j in range(3):
             arrived(ch_part.at[5 + j, two], cx_r.at[1, j])
         ch_part[8, two] = ch_part[1, two] + ch_part[5, two] + ch_part[6, two] + ch_part[7, two]
-        go(ch_part.at[8, two], ch_part.at[9, two], cx_s.at[2, 0], cx_r.at[2, 0], sib, col)
+        go(ch_part.at[8, two], ch_part.at[9, two], cx_s.at[2], cx_r.at[2, 0], sib, col)
+        left(ch.at[0, two], cx_s.at[2])
 
     def chosen_near():
         arrived(ch_part.at[9, two], cx_r.at[2, 0])
         ch[4, two] = ch_part[8, two] + ch_part[9, two]
         for d in range(1, 5):
-            go(ch.at[4, two], ch.at[4 - d, two], z1_s.at[0, d - 1], z1_r.at[0, d - 1], in_z(d), col)
-            go(ch.at[4, two], ch.at[4 + d, two], z1_s.at[1, d - 1], z1_r.at[1, d - 1], in_z(-d), col)
+            go(ch.at[4, two], ch.at[4 - d, two], z1_s.at[0], z1_r.at[0], in_z(d), col)
+            go(ch.at[4, two], ch.at[4 + d, two], z1_s.at[1], z1_r.at[1], in_z(-d), col)
+        left(ch.at[pl.ds(0, 4), two], z1_s.at[0])
+        left(ch.at[pl.ds(0, 4), two], z1_s.at[1])
 
     def chosen_far():
-        for d in range(1, 5):
-            arrived(ch.at[0, two], z1_r.at[0, d - 1])
-            arrived(ch.at[0, two], z1_r.at[1, d - 1])
+        arrived(ch.at[pl.ds(0, 4), two], z1_r.at[0])
+        arrived(ch.at[pl.ds(0, 4), two], z1_r.at[1])
         go(ch.at[pl.ds(0, 4), two], ch.at[pl.ds(12, 4), two], z2_s.at[0], z2_r.at[0], in_z(4), col)
         go(ch.at[pl.ds(5, 3), two], ch.at[pl.ds(9, 3), two], z2_s.at[1], z2_r.at[1], in_z(-4), col)
+        left(ch.at[pl.ds(0, 4), two], z2_s.at[0])
+        left(ch.at[pl.ds(0, 3), two], z2_s.at[1])
 
     held = {"e_sq": jnp.zeros((8, ex.shape[1]), F32), "ch_sq": [jnp.zeros((1, 128), F32)] * 2}
 
@@ -343,11 +353,14 @@
                 kk = (k // 2) * 2 + half if h == 1 else k
                 arrived(view, ring_r.at[h - 1, o, kk])
                 if h < 7 or (far and h < 8):
-                    go(view, piece(after + o * 16, half, k), ring_s.at[h, o, k], ring_r.at[h, o, k], onward, col)
-                go(view, view, sib_s.at[h, o, k], sib_r.at[h], sib, col)
+                    go(view, piece(after + o * 16, half, k), ring_s.at[h], ring_r.at[h, o, k], onward, col)
+                go(view, view, sib_s.at[h], sib_r.at[h], sib, col)
                 for fn in plan.pop((h, event), ()):
                     fn()
                 event += 1
+        if h < 8:
+            left(cand.at[pl.ds(0, 32 if h < 7 else 16)], ring_s.at[h])
+        left(cand.at[pl.ds(0, 32 if h < 8 else 16)], sib_s.at[h])
     assert not plan
     from_sib(7)
     prepare(13)
@@ -374,13 +387,15 @@
 
     def to_sib(p):
         go(g_own.at[1 - c, rows_of(p)], g_sib.at[rows_of(p)], gs_s.at[p], gs_r.at[p], sib, col)
+        left(g_sib.at[rows_of(p)], gs_s.at[p])
 
     def to_levels(p):
         part = rows_of(p)
         arrived(g_sib.at[part], gs_r.at[p])
         g_all[0, part] = g_own[c, part] + g_sib[part]
         for d in (8, 7, 9, 6, 10, 5, 11, 4, 12, 3, 13, 2, 14, 1, 15):
-            go(g_all.at[0, part], g_all.at[d, part], gz_s.at[p, d - 1], gz_r.at[p, d - 1], in_z(d), col)
+            go(g_all.at[0, part], g_all.at[d, part], gz_s.at[p], gz_r.at[p], in_z(d), col)
+        left(g_all.at[pl.ds(1, 15), part], gz_s.at[p])
 
     for p in range(4):
         lax.fori_loop(2 * p, 2 * p + 2, second_half, 0)
@@ -388,20 +403,20 @@
         if p > 0:
             to_levels(p - 1)
     to_levels(3)
+    for copy in sent:
+        copy.wait_send()
     for p in range(4):
-        for d in range(1, LEVELS):
-            arrived(g_all.at[d, rows_of(p)], gz_r.at[p, d - 1])
+        arrived(g_all.at[pl.ds(1, 15), rows_of(p)], gz_r.at[p])
     total = g_all[0]
     for d in range(1, LEVELS):
         total = total + g_all[d]
-    g_sum[c] = total * (1.0 / 32768.0)
+    g_sum[c] = total
     go(g_sum.at[c], g_sum.at[c], gf_s, gf_r, sib, col)
     arrived(g_sum.at[1 - c], gf_r)
     for r in range(2):
         for t in range(16):
             gains_out[pl.ds(r, 1), pl.ds(128 * t, 128)] = g_sum[r, pl.ds(t, 1), :]
-    for copy in pending:
-        copy.wait_send()
+    remote(g_sum.at[c], g_sum.at[c], gf_s, gf_r, sib, col).wait_send()
 
 
 def on_device(example_sketch, candidate_sketch, best_start, chosen):
@@ -443,25 +458,25 @@
             vmem((LEVELS, 16, 128), F32),
             vmem((2, 16, 128), F32),
             dma((4,)),
+            dma((8,)),
             dma((8, 2, PIECES)),
-            dma((8, 2, PIECES)),
-            dma((9, 2, PIECES)),
             dma((9,)),
+            dma((9,)),
+            dma((2, 1)),
             dma((2, 1, 4)),
-            dma((2, 1, 4)),
-            dma((2, 4, 4)),
+            dma((2, 4)),
             dma((2, 4, 4)),
             pltpu.SemaphoreType.REGULAR((3, 2)),
+            dma((3,)),
             dma((3, 3)),
-            dma((3, 3)),
-            dma((2, 4)),
-            dma((2, 4)),
+            dma((2,)),
+            dma((2,)),
             dma((2,)),
             dma((2,)),
             dma((4,)),
             dma((4,)),
-            dma((4, 15)),
-            dma((4, 15)),
+            dma((4,)),
+            dma((4,)),
             dma,
             dma,
         ],
@@ -470,7 +485,7 @@
         ),
         cost_estimate=pl.CostEstimate(flops=6 * 512 * 1024 * 2048, bytes_accessed=300000, transcendentals=4096),
     )(example_sketch, candidate_sketch, best_start.reshape(8, 128), chosen)
-    return best.reshape(examples), gains
+    return jnp.maximum(best.reshape(examples), best_start), gains * (1.0 / 32768.0)
 
 
 def solution(mesh):

time: 70.2 us -> 67.3 us (0.959)
  Pallas kernels: 66.7 us -> 63.8 us
  other arithmetic: 0 us -> 2.6 us
  local copies, waits for them, and re-layouts: 2.59 us -> 0.01 us
    pallas_call x1, Pallas kernels: 66.7 us -> 63.8 us  [on_device(): pl.pallas_call(kernel, out_shape=(jax.ShapeDtypeStruct((8, 128), F32), ja...]
    unnamed x4 -> x2, local copies, waits for them, and re-layouts: 2.59 us -> 0.01 us
    mul x0 -> x1, other arithmetic: none -> 1.33 us  [on_device(): gains * (1.0 / 32768.0)]
    max x0 -> x1, other arithmetic: none -> 1.28 us  [on_device(): jnp.maximum(best.reshape(examples), best_start)]
where the time goes in v3:
time: 67.3 us; the launch traced here: 67.1 us
  Pallas kernels  63.8 us (95%)
  other arithmetic  2.6 us (4%)
    pallas_call x1, Pallas kernels, on_device(): pl.pallas_call(kernel, out_shape=(jax.ShapeDtypeStruct((8, 128), F32), ja...  63.8 us

profile of v3, /device:TPU:1, one launch (start us, length us, event | category | flops | bytes accessed | tf_op | source)
XLA Modules:
  0.0 67.1 jit_solution(64820516309375134)
XLA Ops:
  0.6 0.0 copy-start
  0.6 63.8 %shard_map.59 = (f32[8,128]{1,0:T(8,128)}, f32[2,2048]{1,0:T(2,128)}) custom-call(f32[32,1024]{1,0:T(8,128)} %ex_hbm.1, f32[16,2048]{1,0:T(8,128)} %cand_hbm.1, f32[8,128]{1,0:T(8,128)} %bitcast.3, s32[2]{0:T(128)} %chosen_hbm.1), custom_call_target="tpu_custom_call" | custom-call | flops 6442450944 | bytes 300000 | tf_op jit(solution)/shard_map/pallas_call | solution.py:427
  64.4 0.0 copy-done
  64.5 1.3 %bitcast_maximum_fusion = f32[1024]{0:T(1024)} fusion(f32[1024]{0:T(1024)S(1)} %copy-done, f32[8,128]{1,0:T(8,128)} %get-tuple-element.4), kind=kLoop, calls=%fused_computation.1 | loop fusion | flops 1024 | bytes 12288 | tf_op jit(solution)/shard_map/max | solution.py:488
  65.7 1.3 %broadcast_multiply_fusion = f32[2,2048]{1,0:T(2,128)} fusion(f32[2,2048]{1,0:T(2,128)} %get-tuple-element.5), kind=kLoop, calls=%fused_computation | loop fusion | flops 4096 | bytes 32768 | tf_op jit(solution)/shard_map/mul | solution.py:488
Async XLA Ops:
  0.6 63.8 %copy-start = (f32[1024]{0:T(1024)S(1)}, f32[1024]{0:T(1024)}, u32[]{:S(2)}) copy-start(f32[1024]{0:T(1024)} %param.6) | copy-start | bytes 12292

commit v4 on v3

--- a/solution.py
+++ b/solution.py
@@ -170,6 +170,7 @@
     plan = {}
 
     def at(h, i, *fns):
+        i = 7 if 4 < h < 8 else 3 if h == 8 else i
         plan.setdefault((h, i), []).extend(fns)
 
     def call(fn, *args):
@@ -320,12 +321,12 @@
         at(h + 1, 4, call(prepare, (4 - h) % LEVELS))
         at(h + 1, 5, call(prepare, 4 + h))
     halves = [(n, m) for n in range(8) for m in range(2)]
-    for i, (n, m) in enumerate(halves[:6]):
+    for i, (n, m) in enumerate(halves[:3]):
         at(6, i, call(first_half, n, m))
-    for i, (n, m) in enumerate(halves[6:14]):
+    for i, (n, m) in enumerate(halves[3:8]):
         at(7, i, call(first_half, n, m))
-    for i, (n, m) in enumerate(halves[14:]):
-        at(8, i, call(first_half, n, m))
+    for i, (n, m) in enumerate(halves[8:]):
+        at(8, 3, call(first_half, n, m))
     for i in range(4):
         at(7, 6 + i // 2, call(pick, i))
 
@@ -481,7 +482,7 @@
             dma,
         ],
         compiler_params=pltpu.CompilerParams(
-            collective_id=0, has_side_effects=True, vmem_limit_bytes=60 * 1024 * 1024
+            collective_id=0, has_side_effects=True, vmem_limit_bytes=55200 * 1024
         ),
         cost_estimate=pl.CostEstimate(flops=6 * 512 * 1024 * 2048, bytes_accessed=300000, transcendentals=4096),
     )(example_sketch, candidate_sketch, best_start.reshape(8, 128), chosen)

time: 67.3 us -> 64.8 us (0.963)
  Pallas kernels: 63.8 us -> 61.4 us
  other arithmetic: 2.6 us -> 1.21 us
  local copies, waits for them, and re-layouts: 0.01 us -> 1.33 us
    pallas_call x1, Pallas kernels: 63.8 us -> 61.4 us  [on_device(): pl.pallas_call(kernel, out_shape=(jax.ShapeDtypeStruct((8, 128), F32), ja...]
    unnamed x2 -> x4, local copies, waits for them, and re-layouts: 0.01 us -> 1.33 us
    mul x1, other arithmetic: 1.33 us -> 0.61 us  [on_device(): gains * (1.0 / 32768.0)]
    max x1, other arithmetic: 1.28 us -> 0.6 us  [on_device(): jnp.maximum(best.reshape(examples), best_start)]
where the time goes in v4:
time: 64.8 us; the launch traced here: 64.6 us
  Pallas kernels  61.4 us (95%)
  local copies, waits for them, and re-layouts  1.33 us (2%)
  other arithmetic  1.21 us (2%)
  between operations  0.65 us (1%)
    pallas_call x1, Pallas kernels, on_device(): pl.pallas_call(kernel, out_shape=(jax.ShapeDtypeStruct((8, 128), F32), ja...  61.4 us
    unnamed x4, local copies, waits for them, and re-layouts  1.33 us

profile of v4, /device:TPU:1, one launch (start us, length us, event | category | flops | bytes accessed | tf_op | source)
XLA Modules:
  0.0 64.6 jit_solution(4936548136372378944)
XLA Ops:
  0.6 0.0 copy-start.1
  0.6 0.6 %copy-done.1 = s32[2]{0:T(128)S(1)} copy-done((s32[2]{0:T(128)S(1)}, s32[2]{0:T(128)}, u32[]{:S(2)}) %copy-start.1) | copy-done | bytes 32
  1.3 0.0 copy-start
  1.3 0.7 %copy-done = f32[1024]{0:T(1024)S(1)} copy-done((f32[1024]{0:T(1024)S(1)}, f32[1024]{0:T(1024)}, u32[]{:S(2)}) %copy-start) | copy-done | bytes 4120
  2.0 61.4 %shard_map.59 = (f32[8,128]{1,0:T(8,128)S(1)}, f32[2,2048]{1,0:T(2,128)S(1)}) custom-call(f32[32,1024]{1,0:T(8,128)} %ex_hbm.1, f32[16,2048]{1,0:T(8,128)} %cand_hbm.1, f32[8,128]{1,0:T(8,128)S(1)} %bitcast.3, s32[2]{0:T(128)S(1)} %copy-done.1), custom_call_target="tpu_custom_call" | custom-call | flops 6442450944 | bytes 300000 | tf_op jit(solution)/shard_map/pallas_call | solution.py:428
  63.4 0.6 bitcast_maximum_fusion
  64.0 0.6 broadcast_multiply_fusion
Async XLA Ops:
  0.6 0.7 %copy-start.1 = (s32[2]{0:T(128)S(1)}, s32[2]{0:T(128)}, u32[]{:S(2)}) copy-start(s32[2]{0:T(128)} %chosen_hbm.1) | copy-start | bytes 28
  1.3 0.7 %copy-start = (f32[1024]{0:T(1024)S(1)}, f32[1024]{0:T(1024)}, u32[]{:S(2)}) copy-start(f32[1024]{0:T(1024)} %param.6) | copy-start | bytes 12292

commit v5 on v4

--- a/solution.py
+++ b/solution.py
@@ -33,9 +33,9 @@
 def kernel(
     ex_hbm, cand_hbm, best_hbm, chosen_hbm, best_out, gains_out,
     cand, c_hi, c_lo, c_sq, ex, e_hi, e_lo, acc, best_rep, best_in, chosen, ch_part, ch, ch_hi, ch_lo,
-    g_own, g_sib, g_all, g_sum,
+    g_own, g_sib, g_all, g_alt, g_sum,
     loc_sem, ring_s, ring_r, sib_s, sib_r, p1_s, p1_r, p2_s, p2_r, wave,
-    cx_s, cx_r, z1_s, z1_r, z2_s, z2_r, gs_s, gs_r, gz_s, gz_r, gf_s, gf_r,
+    cx_s, cx_r, z1_s, z1_r, z2_s, z2_r, gs_s, gs_r, gz_s, gz_r, ga_s, ga_r, gf_s, gf_r,
 ):
     row, col = lax.axis_index("row"), lax.axis_index("col")
     z, c, y, x = row // 2, row % 2, col // 4, col % 4
@@ -396,7 +396,12 @@
         g_all[0, part] = g_own[c, part] + g_sib[part]
         for d in (8, 7, 9, 6, 10, 5, 11, 4, 12, 3, 13, 2, 14, 1, 15):
             go(g_all.at[0, part], g_all.at[d, part], gz_s.at[p], gz_r.at[p], in_z(d), col)
+            if p == 3:
+                go(g_all.at[0, part], g_alt.at[d], ga_s, ga_r, in_z(d) + 1 - 2 * c, col)
         left(g_all.at[pl.ds(1, 15), part], gz_s.at[p])
+        if p == 3:
+            go(g_all.at[0, part], g_alt.at[0], ga_s, ga_r, sib, col)
+            left(g_alt, ga_s)
 
     for p in range(4):
         lax.fori_loop(2 * p, 2 * p + 2, second_half, 0)
@@ -406,18 +411,27 @@
     to_levels(3)
     for copy in sent:
         copy.wait_send()
-    for p in range(4):
+    for p in range(3):
         arrived(g_all.at[pl.ds(1, 15), rows_of(p)], gz_r.at[p])
-    total = g_all[0]
+    early = pl.ds(0, 12)
+    total = g_all[0, early]
     for d in range(1, LEVELS):
-        total = total + g_all[d]
-    g_sum[c] = total
-    go(g_sum.at[c], g_sum.at[c], gf_s, gf_r, sib, col)
-    arrived(g_sum.at[1 - c], gf_r)
+        total = total + g_all[d, early]
+    g_sum[c, early] = total
+    go(g_sum.at[c, early], g_sum.at[c, early], gf_s, gf_r, sib, col)
+    arrived(g_sum.at[1 - c, early], gf_r)
+    remote(g_sum.at[c, early], g_sum.at[c, early], gf_s, gf_r, sib, col).wait_send()
+    last = rows_of(3)
+    arrived(g_all.at[pl.ds(1, 15), last], gz_r.at[3])
+    arrived(g_alt, ga_r)
+    total, other = g_all[0, last], g_alt[0]
+    for d in range(1, LEVELS):
+        total, other = total + g_all[d, last], other + g_alt[d]
+    g_sum[c, last] = total
+    g_sum[1 - c, last] = other
     for r in range(2):
         for t in range(16):
             gains_out[pl.ds(r, 1), pl.ds(128 * t, 128)] = g_sum[r, pl.ds(t, 1), :]
-    remote(g_sum.at[c], g_sum.at[c], gf_s, gf_r, sib, col).wait_send()
 
 
 def on_device(example_sketch, candidate_sketch, best_start, chosen):
@@ -457,6 +471,7 @@
             vmem((2, 16, 128), F32),
             vmem((16, 128), F32),
             vmem((LEVELS, 16, 128), F32),
+            vmem((LEVELS, 4, 128), F32),
             vmem((2, 16, 128), F32),
             dma((4,)),
             dma((8,)),
@@ -480,6 +495,8 @@
             dma((4,)),
             dma,
             dma,
+            dma,
+            dma,
         ],
         compiler_params=pltpu.CompilerParams(
             collective_id=0, has_side_effects=True, vmem_limit_bytes=55200 * 1024

time: 64.8 us -> 63.8 us (0.985)
  Pallas kernels: 61.4 us -> 60.5 us
    pallas_call x1, Pallas kernels: 61.4 us -> 60.5 us  [on_device(): pl.pallas_call(kernel, out_shape=(jax.ShapeDtypeStruct((8, 128), F32), ja...]
where the time goes in v5:
time: 63.8 us; the launch traced here: 63.7 us
  Pallas kernels  60.5 us (95%)
  local copies, waits for them, and re-layouts  1.33 us (2%)
  other arithmetic  1.21 us (2%)
  between operations  0.65 us (1%)
    pallas_call x1, Pallas kernels, on_device(): pl.pallas_call(kernel, out_shape=(jax.ShapeDtypeStruct((8, 128), F32), ja...  60.5 us
    unnamed x4, local copies, waits for them, and re-layouts  1.33 us

profile of v5, /device:TPU:1, one launch (start us, length us, event | category | flops | bytes accessed | tf_op | source)
XLA Modules:
  0.0 63.7 jit_solution(13585752569393247094)
XLA Ops:
  0.6 0.0 copy-start.1
  0.6 0.6 %copy-done.1 = s32[2]{0:T(128)S(1)} copy-done((s32[2]{0:T(128)S(1)}, s32[2]{0:T(128)}, u32[]{:S(2)}) %copy-start.1) | copy-done | bytes 32
  1.3 0.0 copy-start
  1.3 0.7 %copy-done = f32[1024]{0:T(1024)S(1)} copy-done((f32[1024]{0:T(1024)S(1)}, f32[1024]{0:T(1024)}, u32[]{:S(2)}) %copy-start) | copy-done | bytes 4120
  2.0 60.5 %shard_map.59 = (f32[8,128]{1,0:T(8,128)S(1)}, f32[2,2048]{1,0:T(2,128)S(1)}) custom-call(f32[32,1024]{1,0:T(8,128)} %ex_hbm.1, f32[16,2048]{1,0:T(8,128)} %cand_hbm.1, f32[8,128]{1,0:T(8,128)S(1)} %bitcast.3, s32[2]{0:T(128)S(1)} %copy-done.1), custom_call_target="tpu_custom_call" | custom-call | flops 6442450944 | bytes 300000 | tf_op jit(solution)/shard_map/pallas_call | solution.py:442
  62.4 0.6 bitcast_maximum_fusion
  63.0 0.6 broadcast_multiply_fusion
Async XLA Ops:
  0.6 0.7 %copy-start.1 = (s32[2]{0:T(128)S(1)}, s32[2]{0:T(128)}, u32[]{:S(2)}) copy-start(s32[2]{0:T(128)} %chosen_hbm.1) | copy-start | bytes 28
  1.3 0.7 %copy-start = (f32[1024]{0:T(1024)S(1)}, f32[1024]{0:T(1024)}, u32[]{:S(2)}) copy-start(f32[1024]{0:T(1024)} %param.6) | copy-start | bytes 12292
